TPU v7x, 256 devices: a whole 4x4x8 slice. The times are simulated.
256 devices in a mesh: group: 4 (over x_hi, core), shard: 64 (over y, z, x_lo).
Axes of the slice: x: 4 (x_hi: 2, x_lo: 2; x = x_hi * 2 + x_lo), y: 4, z: 8, core: 2. Of those that a mesh axis runs over, the one named last changes fastest.
Arguments:
- queries: bfloat16 [16, 16, 5120], P('group'), may hold values from -150 to 150
- fresh_kv: bfloat16 [2, 16, 16, 1024], P(None, 'group'), may hold values from -4.5 to 4.5
- kv_pages: bfloat16 [2, 256, 128, 1024], P(None, ('group', 'shard')), may hold values from -4.5 to 4.5
- page_list: int32 [16, 64], P('group'), may hold values from 0 to 255, as said below
- tile_mask: int32 [16, 64], P('group'), may hold values from 0 to 1, as said below
- out_weight: bfloat16 [5120, 5120], P('shard'), may hold values from -0.078125 to 0.078125
Outputs:
- block_output: bfloat16 [16, 16, 5120], P('group', None, 'shard')
Inputs may be any that keep to these rules, and one draw needn't show every extreme that they name: `page_list`: each branch's 64 page numbers are different. `tile_mask`: the valid slots of a branch are the first 16 to 64 of its list; some branch has all 64 valid.
All inputs are finite; a program needn't handle non-finite values.
Results may differ from a plain program's by a relative error of at most 0.03.
Values may be sent and summed in bfloat16 or wider, within the bound.
A program may use at most 192 MiB of HBM per device.

v0:
```python
import math

import jax
import jax.numpy as jnp
from jax import lax
from jax.sharding import PartitionSpec as P

KV_HEADS = 8


NEG_FILL = -1e30


def masked_state(scores, visible):
    masked = jnp.where(visible, scores, NEG_FILL)
    highest = jnp.max(masked, axis=-1)
    weights = jnp.where(visible, jnp.exp(masked - highest[..., None]), 0.0)
    return (highest, jnp.sum(weights, axis=-1), weights.astype(jnp.bfloat16))


def combine(left_state, right_state):
    left_peak, left_sum, left_acc = left_state
    right_peak, right_sum, right_acc = right_state
    joined = jnp.maximum(left_peak, right_peak)
    left_scale = jnp.exp(left_peak - joined)
    right_scale = jnp.exp(right_peak - joined)
    return (
        joined,
        left_sum * left_scale + right_sum * right_scale,
        left_acc * left_scale[..., None] + right_acc * right_scale[..., None],
    )


def page_state(query_rows, key_rows, value_rows, allowed, kv_heads):
    branch_rows, block_len, q_width = query_rows.shape
    head_dim = key_rows.shape[1] // kv_heads
    group_size = q_width // (head_dim * kv_heads)
    scaling = 1.0 / math.sqrt(head_dim)
    query_heads = jnp.moveaxis(
        query_rows.reshape(branch_rows, block_len, kv_heads, group_size, head_dim), 2, 0
    )
    key_heads = jnp.moveaxis(key_rows.reshape(-1, kv_heads, head_dim), 1, 0)
    value_heads = jnp.moveaxis(value_rows.reshape(-1, kv_heads, head_dim), 1, 0)
    visible = allowed[:, None, None, :]

    def per_head(items):
        query_head, key_head, value_head = items
        scores = (
            jnp.einsum("rcgd,nd->rcgn", query_head, key_head, preferred_element_type=jnp.float32)
            * scaling
        )
        highest, totals, rounded = masked_state(scores, visible)
        summed = jnp.einsum(
            "rcgn,nd->rcgd", rounded, value_head, preferred_element_type=jnp.float32
        )
        return (highest, totals, summed)

    return lax.map(per_head, (query_heads, key_heads, value_heads))


def block_state(query_rows, fresh_kv, is_first, kv_heads):
    branch_rows, block_len, q_width = query_rows.shape
    kv_width = fresh_kv.shape[-1]
    head_dim = kv_width // kv_heads
    group_size = q_width // kv_width
    scaling = 1.0 / math.sqrt(head_dim)
    query_heads = query_rows.reshape(branch_rows, block_len, kv_heads, group_size, head_dim)
    key_heads = fresh_kv[0].reshape(branch_rows, block_len, kv_heads, head_dim)
    value_heads = fresh_kv[1].reshape(branch_rows, block_len, kv_heads, head_dim)
    scores = (
        jnp.einsum("rchgd,rnhd->hrcgn", query_heads, key_heads, preferred_element_type=jnp.float32)
        * scaling
    )
    positions = jnp.arange(block_len)
    visible = ((positions[None, :] <= positions[:, None]) & is_first)[None, None, :, None, :]
    highest, totals, rounded = masked_state(scores, visible)
    summed = jnp.einsum(
        "hrcgn,rnhd->hrcgd", rounded, value_heads, preferred_element_type=jnp.float32
    )
    return (highest, totals, summed)


def member(page_ids, page_valid, numbers):
    return jnp.any(
        (page_ids[:, :, None] == numbers[None, None, :]) & (page_valid[:, :, None] > 0), axis=1
    )


def layout(weighted):
    moved = jnp.moveaxis(weighted, 0, 2)
    return moved.reshape(moved.shape[0], moved.shape[1], -1)


def on_device(queries, fresh_kv, kv_pages, page_list, tile_mask, out_weight):
    branch_rows, block_len, q_width = queries.shape
    local_count = kv_pages.shape[1]
    page_len = kv_pages.shape[2]
    kv_width = kv_pages.shape[3]
    shard_count = lax.axis_size("shard")
    shard_at = lax.axis_index("shard")
    is_first = shard_at == 0
    slice_width = q_width // shard_count
    own_state = block_state(queries, fresh_kv, is_first, KV_HEADS)
    piece = lax.all_gather(kv_pages, "group", axis=1, tiled=True)
    piece_count = piece.shape[1]
    positions = jnp.arange(piece_count, dtype=jnp.int32)
    numbers = (
        positions // local_count * shard_count + shard_at
    ) * local_count + positions % local_count
    allowed = jnp.repeat(member(page_list, tile_mask, numbers), page_len, axis=1)
    fresh_state = page_state(
        queries,
        piece[0].reshape(piece_count * page_len, kv_width),
        piece[1].reshape(piece_count * page_len, kv_width),
        allowed,
        KV_HEADS,
    )
    gathered_state = combine(own_state, fresh_state)
    peak_local, sum_local, weighted = gathered_state
    peak_all = lax.pmax(peak_local, "shard")
    rescale = jnp.exp(peak_local - peak_all)
    sum_all = lax.psum(sum_local * rescale, "shard")
    terms = layout(weighted * (rescale / sum_all)[..., None])
    attention = lax.psum_scatter(terms, "shard", scatter_dimension=2, tiled=True)
    attention = attention.astype(jnp.bfloat16)
    projected = jnp.dot(
        attention.reshape(branch_rows * block_len, slice_width),
        out_weight,
        preferred_element_type=jnp.float32,
    ).reshape(branch_rows, block_len, -1)
    return lax.psum_scatter(projected, "shard", scatter_dimension=2, tiled=True).astype(
        jnp.bfloat16
    )


def solution(mesh):
    return jax.shard_map(
        on_device,
        mesh=mesh,
        in_specs=(
            P("group", None, None),
            P(None, "group", None, None),
            P(None, ("group", "shard"), None, None),
            P("group", None),
            P("group", None),
            P("shard", None),
        ),
        out_specs=P("group", None, "shard"),
        check_vma=False,
    )
```

profile of v0, /device:TPU:4, one launch (start us, length us, event | category | flops | bytes accessed | tf_op | source)
XLA Modules:
  0.0 1344.5 jit_solution(5486141208081700750)
XLA Ops:
  6.5 0.7 all-gather.2.cloned.1.call-update
  7.3 1.0 fusion.40
  8.4 0.8 reshape.37
  9.2 0.8 copy.42
  10.3 1.4 fusion.41
  11.8 1.0 copy-done.1
  12.8 0.4 fusion.23
  13.2 0.7 bitcast_bitcast_fusion
  13.9 24.7 %all-gather.2.cloned.1.call-done = bf16[2,4,128,1024]{3,2,1,0:T(8,128)(2,1)} async-done(((bf16[2,1,128,1024]{3,2,1,0:T(8,128)(2,1)}), bf16[2,4,128,1024]{3,2,1,0:T(8,128)(2,1)}) %all-gather.2.cloned.1.call-update) | async-done | bytes 2097168 | tf_op jit(solution)/shard_map/all_gather | solution.py:104
  38.6 1.7 fusion.39
  40.4 0.3 copy.65
  40.6 1.2 copy.44
  41.8 0.3 copy.64
  42.2 20.6 %while.15 = (s32[]{:T(128)}, f32[8,4,16,5]{2,3,1,0:T(8,128)S(1)}, f32[8,4,16,5]{2,3,1,0:T(8,128)S(1)}, f32[8,4,16,5,128]{4,2,3,1,0:T(8,128)}, bf16[8,4,16,5,128]...) while((s32[]{:T(128)}, f32[8,4,16,5]{2,3,1,0:T(8,128)S(1)}, ...), condition=%wide.region_5.6_spmd.clone, body=%wide.region_2.5_spmd.clone.sunk | while | flops 85360000 | bytes 2559097 | solution.py:58
  42.3 0.3 fusion.50
  42.6 0.3 fusion.51
  42.9 1.9 fusion.52
  44.9 0.3 fusion.50
  45.2 0.3 fusion.51
  45.5 1.9 fusion.52
  47.5 0.3 fusion.50
  48.1 1.9 fusion.52
  50.1 0.3 fusion.50
  50.7 1.9 fusion.52
  52.6 0.3 fusion.50
  53.0 0.3 fusion.51
  53.3 1.9 fusion.52
  55.2 0.3 fusion.50
  55.5 0.3 fusion.51
  55.8 1.9 fusion.52
  57.8 0.3 fusion.50
  58.4 1.9 fusion.52
  60.4 0.3 fusion.50
  61.0 1.9 fusion.52
  62.9 310.1 %pmax.7 = f32[8,4,16,5]{2,3,1,0:T(8,128)S(1)} all-reduce(f32[8,4,16,5]{2,3,1,0:T(8,128)S(1)} %max.5), channel_id=1, replica_groups=mesh['group'=4,'shard'=64] {'shard'}, use_global_device_ids=true, to_apply=%region_6.7 | all-reduce | flops 2560 | bytes 20480 | tf_op jit(solution)/shard_map/pmax | solution.py:120
  373.0 0.8 add_multiply_fusion
  373.8 302.7 %psum.7 = f32[8,4,16,5]{2,3,1,0:T(8,128)S(1)} all-reduce(f32[8,4,16,5]{2,3,1,0:T(8,128)S(1)} %get-tuple-element.119), channel_id=1, replica_groups=mesh['group'=4,'shard'=64] {'shard'}, use_global_device_ids=true, to_apply=%region_8.9 | all-reduce | flops 2560 | bytes 20480 | tf_op jit(solution)/shard_map/psum | solution.py:122
  676.5 2.7 fusion.22
  679.2 6.5 copy.59
  685.7 8.9 reshape.45
  694.7 312.4 %reduce-scatter.7.cloned.1.call-done = f32[80,64]{1,0:T(8,128)} async-done(((f32[5120,64]{1,0:T(8,128)}), f32[80,64]{1,0:T(8,128)}) %reduce-scatter.7.cloned.1.call-update) | async-done | bytes 20496
  1007.2 0.9 reshape.46
  1008.2 0.3 fusion.25
  1008.5 6.5 copy.57
  1015.0 8.9 reshape.47
  1023.9 312.4 %reduce-scatter.9.cloned.1.call-done = f32[80,64]{1,0:T(8,128)} async-done(((f32[5120,64]{1,0:T(8,128)}), f32[80,64]{1,0:T(8,128)}) %reduce-scatter.9.cloned.1.call-update) | async-done | bytes 20496
  1336.4 0.9 reshape.48
  1337.3 0.7 copy.58
  (60 shorter events, 2.5 us)
Async XLA Ops:
  6.5 1001.6 %copy-start = (bf16[80,5120]{1,0:T(8,128)(2,1)S(1)}, bf16[80,5120]{1,0:T(8,128)(2,1)}, u32[]{:S(2)}) copy-start(bf16[80,5120]{1,0:T(8,128)(2,1)} %param.13) | copy-start | bytes 2457604
  6.5 1.9 copy-start.4
  6.5 32.1 %all-gather.2.cloned.1.call-start = ((), (), s32[]{:S(2)}) async-start(), calls=%async_computation.2 | async-start | bytes 2621440 | tf_op jit(solution)/shard_map/all_gather | solution.py:104
  7.3 999.9 %reduce-scatter.7.cloned.1.call-start = ((), (), s32[]{:S(2)}) async-start(), calls=%async_computation.3 | async-start | bytes 2662400
  8.4 1.6 copy-start.5
  8.4 1.6 copy-start.6
  11.7 1.1 copy-start.1
  11.7 361.3 %copy-start.3 = (f32[8,4,16,5]{2,3,1,0:T(8,128)}, f32[8,4,16,5]{2,3,1,0:T(8,128)S(1)}, u32[]{:S(2)}) copy-start(f32[8,4,16,5]{2,3,1,0:T(8,128)S(1)} %get-tuple-element.130) | copy-start | bytes 30724
  62.9 613.7 %copy-start.2 = (f32[8,4,16,5,16]{2,4,3,1,0:T(8,128)S(1)}, f32[8,4,16,5,16]{2,4,3,1,0:T(8,128)}, u32[]{:S(2)}) copy-start(f32[8,4,16,5,16]{2,4,3,1,0:T(8,128)} %copy-done.1) | copy-start | bytes 491524
  694.7 641.7 %reduce-scatter.9.cloned.1.call-start = ((), (), s32[]{:S(2)}) async-start(), calls=%async_computation.4 | async-start | bytes 2662400
Sparse Core Ops, SparseCore 0:
  9.2 29.4 all-gather.1
  694.8 312.3 reduce-scatter.6
  1024.1 312.2 reduce-scatter.8
where the time goes:
time: 1350 us; the launch traced here: 1340 us
  waiting for transfers between devices  650 us (48%)
  blocking collectives  613 us (45%)
  local copies, waits for them, and re-layouts  42.1 us (3%)
  matrix products  22.1 us (2%)
    unnamed x5, waiting for transfers between devices  626 us
    pmax x1, blocking collectives, on_device(): peak_all = lax.pmax(peak_local, 'shard')  310 us
    psum x1, blocking collectives, on_device(): sum_all = lax.psum(sum_local * rescale, 'shard')  303 us
    unnamed x29, local copies, waits for them, and re-layouts  37.2 us
  transfers between devices with their start and end apart: 3, of which 3 were waited for; matrix products, arithmetic and copies ran while one was open for 0% of the time, Pallas kernels for 0%

commit v1 on v0

v1 whole, which is shorter than its diff:
```python
import functools
import math

import jax
import jax.numpy as jnp
from jax import lax
from jax.experimental import pallas as pl
from jax.experimental.pallas import tpu as pltpu
from jax.sharding import PartitionSpec as P

MESH = pl.DeviceIdType.MESH
BF, F32 = jnp.bfloat16, jnp.float32
HIDDEN = -1e30
FLOOR = -1e29


def device(h, m, y, z, c):
    return (h * 2 + c, (y * 8 + z) * 2 + (m + h) % 2)


def kernel(
    q_hbm, f_hbm, kv_hbm, list_ref, mask_ref, w_hbm, out_ref,
    qb, qc, kvb, fb, eb, bias, m_ref, l_ref, acc, wv, wp, wb,
    accs, sts, accr, strv, attp, att_t, os, orv,
    loc, pg_s, pg_r, fw_s, fw_r, q_s, q_r, w_s, w_r, wf_s, wf_r,
    ac_s, ac_r, st_s, st_r, at_s, at_r, o_s, o_r,
):
    g = lax.axis_index("group")
    s = lax.axis_index("shard")
    h, c = g // 2, g % 2
    y, z, l = s // 16, (s // 2) % 8, s % 2
    m = (l + h) % 2
    head = 2 * y + m
    plane = [(dm, dy) for dm in range(2) for dy in range(4)]
    column = [(dh, dz) for dh in range(2) for dz in range(8)]
    sibling = device(h, m, y, z, 1 - c)
    across = device(1 - h, m, y, z, c)

    def in_plane(j):
        dm, dy = plane[j]
        return device(h, (m + dm) % 2, (y + dy) % 4, z, c)

    def in_column(k):
        dh, dz = column[k]
        return device((h + dh) % 2, m, y, (z + dz) % 8, c)

    def w_to(k):
        return z // 4, 2 * k + (z + c) % 2

    def w_from(k):
        return (k % 2 + h) % 2, 4 * m + 2 * (k // 2) + (z + c) % 2

    def w_slot(zz, ll):
        return (zz % 4) * 2 + ll

    bar = pltpu.get_barrier_semaphore()

    def greet(d):
        pl.semaphore_signal(bar, inc=1, device_id=d, device_id_type=MESH)

    greet(sibling)
    for j in range(1, 8):
        greet(in_plane(j))
    for k in range(1, 16):
        greet(in_column(k))
    for k in range(4):
        m2, z2 = w_from(k)
        pl.when((m2 != m) | (z2 != z))(functools.partial(greet, device(h, m2, y, z2, c)))
    w_self = (z // 4 == m) & (c == 0)

    cols = pl.ds(pl.multiple_of(head * 128, 128), 128)
    q_cols = pl.ds(pl.multiple_of(head * 640, 128), 640)
    ld_q = pltpu.make_async_copy(q_hbm.at[:, q_cols], qb.at[0], loc.at[0])
    ld_kv = pltpu.make_async_copy(kv_hbm.at[:, :, cols], kvb.at[:, 0], loc.at[1])
    ld_f = pltpu.make_async_copy(f_hbm.at[:, :, cols], fb, loc.at[2])
    ld_w = pltpu.make_async_copy(w_hbm, wv, loc.at[3])
    ld_w.start()
    ld_q.start()
    ld_kv.start()
    ld_f.start()

    eb[0] = jnp.full((8, 128), -1, jnp.int32)
    eb[0, 0:4, 0:64] = jnp.where(mask_ref[...] > 0, list_ref[...], -1)

    ld_w.wait()
    for z2 in range(8):
        wp[z2] = jnp.concatenate(
            [wv[:, 1280 * y2 + 160 * z2 : 1280 * y2 + 160 * z2 + 160] for y2 in range(4)], axis=1
        )

    pl.semaphore_wait(bar, 27 - w_self.astype(jnp.int32))

    def send(src, dst, ss, rs, d):
        cp = pltpu.make_async_remote_copy(
            src_ref=src, dst_ref=dst, send_sem=ss, recv_sem=rs, device_id=d, device_id_type=MESH
        )
        cp.start()
        return cp

    sent = []
    snd_e = send(eb.at[0], eb.at[1], q_s.at[0], q_r.at[0], across)
    pages = [None] * 8
    for j in (6, 2, 7, 5, 3, 1, 4):
        dm, dy = plane[j]
        there = 2 * ((y + dy) % 4) + (m + dm) % 2
        there_cols = pl.ds(pl.multiple_of(there * 128, 128), 128)
        pages[j] = send(kv_hbm.at[:, :, there_cols], kvb.at[:, j], pg_s.at[j], pg_r.at[j], in_plane(j))
    ld_q.wait()
    snd_q = send(qb.at[0], qb.at[1], q_s.at[1], q_r.at[1], across)
    ld_kv.wait()
    forwards = [None] * 8
    forwards[0] = send(kvb.at[:, 0], kvb.at[:, 8], fw_s.at[0], fw_r.at[0], sibling)

    for k in range(4):
        m2, z2 = w_to(k)
        here = (m2 == m) & (z2 == z)
        rows = pl.ds(pl.multiple_of(80 * w_slot(z, l), 16), 80)
        slot = ((z % 4) // 2) * 2 + l

        @pl.when(here)
        def _():
            pltpu.make_async_copy(wp.at[z2], wb.at[rows], loc.at[4]).start()

        @pl.when(jnp.logical_not(here))
        def _():
            send(wp.at[z2], wb.at[rows], w_s.at[k], w_r.at[slot], device(h, m2, y, z2, c))

    snd_e.wait_recv()
    lists = eb[...].reshape(16, 128)
    row = lax.broadcasted_iota(jnp.int32, (16, 640), 0)
    col = lax.broadcasted_iota(jnp.int32, (16, 640), 1)
    owner = jnp.where(col >= 320, 8, 0) + ((col >> 4) & 3)
    pick = (row == owner).astype(F32)
    for j in range(16):
        dm, dy = plane[j % 8]
        src_m, src_y, src_c = (m - dm + 2) % 2, (y - dy + 4) % 4, (c + j // 8) % 2
        src_l = (src_m + h) % 2
        number = (h * 2 + src_c) * 64 + (src_y * 8 + z) * 2 + src_l
        seen = jnp.max((lists == number).astype(F32), axis=1, keepdims=True)
        bias[pl.ds(j, 1), :] = (jnp.sum(pick * seen, axis=0, keepdims=True) - 1.0) * (-HIDDEN)

    snd_q.wait_recv()
    for o in range(2):
        for i in range(5):
            qc[o * 320 + i * 64 : o * 320 + i * 64 + 64, :] = qb[o, :, i * 128 : i * 128 + 128]

    scale = math.log2(math.e) / math.sqrt(128)

    def scores(keys):
        return lax.dot_general(keys, qc[...], (((1,), (1,)), ((), ())), preferred_element_type=F32) * scale

    def weigh(values, weights):
        return lax.dot_general(
            values, weights.astype(BF), (((0,), (0,)), ((), ())), preferred_element_type=F32
        )

    ld_f.wait()
    key = lax.broadcasted_iota(jnp.int32, (64, 640), 0)
    col = lax.broadcasted_iota(jnp.int32, (64, 640), 1)
    visible = (col < 320) & ((key >> 4) == ((col >> 4) & 3)) & ((key & 15) <= (col & 15)) & (z == 0)
    sc = jnp.where(visible, scores(fb[0]), HIDDEN)
    top = jnp.maximum(jnp.max(sc, axis=0, keepdims=True), FLOOR)
    wt = jnp.exp2(sc - top)
    m_ref[...] = top
    l_ref[...] = jnp.sum(wt, axis=0, keepdims=True)
    acc[...] = weigh(fb[1], wt)

    def block(first):
        sc = scores(kvb[0, first : first + 4].reshape(512, 128))
        sc = (sc.reshape(4, 128, 640) + bias[first : first + 4, :][:, None, :]).reshape(512, 640)
        old = m_ref[...]
        top = jnp.maximum(old, jnp.max(sc, axis=0, keepdims=True))
        keep = jnp.exp2(old - top)
        wt = jnp.exp2(sc - top)
        m_ref[...] = top
        l_ref[...] = l_ref[...] * keep + jnp.sum(wt, axis=0, keepdims=True)
        acc[...] = acc[...] * keep + weigh(kvb[1, first : first + 4].reshape(512, 128), wt)

    def pass_on(j):
        pages[j].wait_recv()
        forwards[j] = send(kvb.at[:, j], kvb.at[:, 8 + j], fw_s.at[j], fw_r.at[j], sibling)

    for j in (1, 3, 2):
        pass_on(j)
    block(0)
    for j in (4, 5, 7, 6):
        pass_on(j)
    for j in range(4):
        forwards[j].wait_recv()
    block(8)
    block(4)
    for j in range(4, 8):
        forwards[j].wait_recv()
    block(12)

    nil = jnp.zeros((128, 64), F32)
    for o in range(2):
        at = slice(o * 320, o * 320 + 320)
        accs[o] = jnp.concatenate([acc[:, at], nil], axis=1).astype(BF)
        sts[o] = jnp.concatenate(
            [jnp.concatenate([m_ref[:, at], l_ref[:, at]], axis=0), nil[0:2]], axis=1
        )
    parts, stats = [None] * 16, [None] * 16
    for k in (12, 4, 11, 13, 3, 5, 10, 14, 2, 6, 9, 15, 1, 7, 8):
        dh, dz = column[k]
        rows = pl.ds(pl.multiple_of(16 * ((z + dz) % 8), 16), 16)
        stats[k] = send(sts.at[dh], strv.at[k], st_s.at[k], st_r.at[k], in_column(k))
        parts[k] = send(accs.at[dh, rows], accr.at[k], ac_s.at[k], ac_r.at[k], in_column(k))
    mine = pl.ds(pl.multiple_of(16 * z, 16), 16)
    accr[0] = accs[0, mine, :]
    strv[0] = sts[0]

    w_fwd = []
    for k in range(4):
        m2, z2 = w_from(k)
        here = (m2 == m) & (z2 == z)
        rows = pl.ds(pl.multiple_of(80 * w_slot(z2, k % 2), 16), 80)

        @pl.when(here)
        def _():
            pltpu.make_async_copy(wp.at[z2], wb.at[rows], loc.at[4]).wait()

        @pl.when(jnp.logical_not(here))
        def _():
            pltpu.make_async_remote_copy(
                src_ref=wp.at[0], dst_ref=wb.at[rows], send_sem=w_s.at[k], recv_sem=w_r.at[k],
                device_id=sibling, device_id_type=MESH,
            ).wait_recv()

        w_fwd.append(send(wb.at[rows], wb.at[rows], wf_s.at[k], wf_r.at[k], sibling))

    for k in range(1, 16):
        stats[k].wait_recv()
    tops, sums = strv[:, 0, :], strv[:, 1, :]
    top = jnp.max(tops, axis=0, keepdims=True)
    factor = jnp.exp2(tops - top)
    factor = factor / jnp.sum(factor * sums, axis=0, keepdims=True)
    total = jnp.zeros((16, 384), F32)
    for k in range(16):
        if k:
            parts[k].wait_recv()
        total = total + accr[k].astype(F32) * factor[k : k + 1, :]
    attp[...] = total.astype(BF)

    gathered = [None] * 8
    for dz in (4, 3, 5, 2, 6, 1, 7):
        gathered[dz] = send(attp, att_t.at[mine], at_s.at[dz], at_r.at[dz], in_column(dz))
    att_t[mine, :] = attp[...]
    for k in range(4):
        w_fwd[k].wait_recv()
    for dz in range(1, 8):
        gathered[dz].wait_recv()

    att = att_t[...].astype(F32).T.astype(BF)
    proj = jnp.zeros((64, 640), F32)
    for i in range(5):
        proj += jnp.dot(att[i * 64 : i * 64 + 64], wb[i * 128 : i * 128 + 128, :], preferred_element_type=F32)
    for k in range(8):
        os[k] = jnp.concatenate([proj[:, 80 * k : 80 * k + 80], jnp.zeros((64, 48), F32)], axis=1).astype(BF)
    outs = [None] * 8
    for j in (6, 2, 7, 5, 3, 1, 4):
        dm, dy = plane[j]
        k = 2 * ((y + dy) % 4) + ((m + dm) % 2 + h) % 2
        outs[j] = send(os.at[k], orv.at[j], o_s.at[j], o_r.at[j], in_plane(j))
    result = os[2 * y + l].astype(F32)
    for j in range(1, 8):
        outs[j].wait_recv()
        result += orv[j].astype(F32)
    out_ref[...] = result[:, :80].astype(BF)

    snd_e.wait_send()
    snd_q.wait_send()
    for j in range(8):
        if j:
            pages[j].wait_send()
            outs[j].wait_send()
            gathered[j].wait_send()
        forwards[j].wait_send()
    for k in range(1, 16):
        stats[k].wait_send()
        parts[k].wait_send()
    for k in range(4):
        w_fwd[k].wait_send()
        m2, z2 = w_to(k)

        @pl.when((m2 != m) | (z2 != z))
        def _():
            pltpu.make_async_remote_copy(
                src_ref=wp.at[z2], dst_ref=wb.at[pl.ds(0, 80)], send_sem=w_s.at[k], recv_sem=w_r.at[k],
                device_id=sibling, device_id_type=MESH,
            ).wait_send()


def on_device(queries, fresh_kv, kv_pages, page_list, tile_mask, out_weight):
    any_spec, vmem = pl.BlockSpec(memory_space=pl.ANY), pl.BlockSpec(memory_space=pltpu.VMEM)
    sem = lambda n: pltpu.SemaphoreType.DMA((n,))
    out = pl.pallas_call(
        kernel,
        out_shape=jax.ShapeDtypeStruct((64, 80), BF),
        in_specs=[any_spec, any_spec, any_spec, vmem, vmem, any_spec],
        out_specs=vmem,
        scratch_shapes=[
            pltpu.VMEM((2, 64, 640), BF),
            pltpu.VMEM((640, 128), BF),
            pltpu.VMEM((2, 16, 128, 128), BF),
            pltpu.VMEM((2, 64, 128), BF),
            pltpu.VMEM((2, 8, 128), jnp.int32),
            pltpu.VMEM((16, 640), F32),
            pltpu.VMEM((1, 640), F32),
            pltpu.VMEM((1, 640), F32),
            pltpu.VMEM((128, 640), F32),
            pltpu.VMEM((80, 5120), BF),
            pltpu.VMEM((8, 80, 640), BF),
            pltpu.VMEM((640, 640), BF),
            pltpu.VMEM((2, 128, 384), BF),
            pltpu.VMEM((2, 2, 384), F32),
            pltpu.VMEM((16, 16, 384), BF),
            pltpu.VMEM((16, 2, 384), F32),
            pltpu.VMEM((16, 384), BF),
            pltpu.VMEM((128, 384), BF),
            pltpu.VMEM((8, 64, 128), BF),
            pltpu.VMEM((8, 64, 128), BF),
            sem(5), sem(8), sem(8), sem(8), sem(8), sem(2), sem(2), sem(4), sem(4), sem(4), sem(4),
            sem(16), sem(16), sem(16), sem(16), sem(8), sem(8), sem(8), sem(8),
        ],
        compiler_params=pltpu.CompilerParams(
            collective_id=0, has_side_effects=True, vmem_limit_bytes=40 * 2**20
        ),
        name="attend",
    )(
        queries.reshape(64, 5120),
        fresh_kv.reshape(2, 64, 1024),
        kv_pages.reshape(2, 128, 1024),
        page_list,
        tile_mask,
        out_weight,
    )
    return out.reshape(4, 16, 80)


def solution(mesh):
    return jax.shard_map(
        on_device,
        mesh=mesh,
        in_specs=(
            P("group", None, None),
            P(None, "group", None, None),
            P(None, ("group", "shard"), None, None),
            P("group", None),
            P("group", None),
            P("shard", None),
        ),
        out_specs=P("group", None, "shard"),
        check_vma=False,
    )
```

time: 1350 us -> 48.4 us (0.04)
  waiting for transfers between devices: 650 us -> 0 us
  blocking collectives: 613 us -> 0 us
  Pallas kernels: 0 us -> 42.1 us
  local copies, waits for them, and re-layouts: 42.1 us -> 5.53 us
  matrix products: 22.1 us -> 0 us
    unnamed x5 -> x0, waiting for transfers between devices: 626 us -> none
    pmax x1 -> x0, blocking collectives: 310 us -> none  [on_device(): peak_all = lax.pmax(peak_local, 'shard')]
    psum x1 -> x0, blocking collectives: 303 us -> none  [on_device(): sum_all = lax.psum(sum_local * rescale, 'shard')]
    pallas_call x0 -> x1, Pallas kernels: none -> 42.1 us  [on_device(): pl.pallas_call(kernel, out_shape=jax.ShapeDtypeStruct((64, 80), BF), in_s...]
    unnamed x29 -> x13, local copies, waits for them, and re-layouts: 37.2 us -> 5.53 us
    all_gather x1 -> x0, waiting for transfers between devices: 24.7 us -> none  [on_device(): piece = lax.all_gather(kv_pages, 'group', axis=1, tiled=True)]
    dot_general x19 -> x0, matrix products: 22.1 us -> none  [the longest x8 15 us: per_head(): jnp.einsum('rcgn,nd->rcgd', rounded, value_head, preferred_element_type=j...]
  transfers between devices with their start and end apart: 3 -> 0, of which waited for: 3 -> 0; matrix products, arithmetic and copies ran while one was open for 0% -> 0% of each run, Pallas kernels for 0% -> 0%
where the time goes in v1:
time: 48.4 us; the launch traced here: 47.7 us
  Pallas kernels  42.1 us (87%)
  local copies, waits for them, and re-layouts  5.53 us (11%)
    pallas_call x1, Pallas kernels, on_device(): pl.pallas_call(kernel, out_shape=jax.ShapeDtypeStruct((64, 80), BF), in_s...  42.1 us
    unnamed x13, local copies, waits for them, and re-layouts  5.53 us

profile of v1, /device:TPU:4, one launch (start us, length us, event | category | flops | bytes accessed | tf_op | source)
XLA Modules:
  0.0 47.7 jit_solution(11115472915253610557)
XLA Ops:
  0.0 0.0 copy-start.5
  0.0 0.0 copy-start.4
  0.0 0.7 %copy-done.5 = s32[4,64]{1,0:T(4,128)S(1)} copy-done((s32[4,64]{1,0:T(4,128)S(1)}, s32[4,64]{1,0:T(4,128)}, u32[]{:S(2)}) %copy-start.5) | copy-done | bytes 1048
  0.7 0.0 copy-done.4
  0.7 0.0 copy-start
  0.7 1.1 %copy-done = bf16[80,5120]{1,0:T(8,128)(2,1)S(1)} copy-done((bf16[80,5120]{1,0:T(8,128)(2,1)S(1)}, bf16[80,5120]{1,0:T(8,128)(2,1)}, u32[]{:S(2)}) %copy-start) | copy-done | bytes 819224
  1.8 0.0 copy-start.1
  1.8 1.1 %copy-done.1 = bf16[4,16,5120]{2,1,0:T(8,128)(2,1)S(1)} copy-done((bf16[4,16,5120]{2,1,0:T(8,128)(2,1)S(1)}, bf16[4,16,5120]{2,1,0:T(8,128)(2,1)}, u32[]{:S(2)}) %copy-start.1) | copy-done | bytes 655384
  2.9 0.0 copy-start.2
  2.9 1.0 %copy-done.2 = bf16[2,1,128,1024]{3,2,1,0:T(8,128)(2,1)S(1)} copy-done((bf16[2,1,128,1024]{3,2,1,0:T(8,128)(2,1)S(1)}, bf16[2,1,128,1024]{3,2,1,0:T(8,128)(2,1)}, u32[]{:S(2)}) %copy-start.2) | copy-done | bytes 524312
  4.0 0.0 copy-start.3
  4.0 0.9 %copy-done.3 = bf16[2,4,16,1024]{3,2,1,0:T(8,128)(2,1)S(1)} copy-done((bf16[2,4,16,1024]{3,2,1,0:T(8,128)(2,1)S(1)}, bf16[2,4,16,1024]{3,2,1,0:T(8,128)(2,1)}, u32[]{:S(2)}) %copy-start.3) | copy-done | bytes 262168
  4.9 42.1 %attend.1 = bf16[64,80]{1,0:T(8,128)(2,1)S(1)} custom-call(bf16[64,5120]{1,0:T(8,128)(2,1)S(1)} %bitcast.4, bf16[2,64,1024]{2,1,0:T(8,128)(2,1)S(1)} %bitcast.6, bf16[2,128,1024]{2,1,0:T(8,128)(2,1)S(1)} %bitcast.5, s32[4,64]{1,0:T(4,128)S(1)} %copy-done.4, s32[4,64]{1,0:T(4,128)S(1)} %copy-done.5, bf16[80,5120]{1,0:T(8,128)(2,1)S(1)} %copy-done), custom_call_target="tpu_custom_call" | custom-call | tf_op jit(solution)/shard_map/attend/pallas_call | solution.py:297
  47.1 0.6 %copy.8 = bf16[4,16,80]{2,1,0:T(8,128)(2,1)} copy(bf16[4,16,80]{2,1,0:T(8,128)(2,1)S(1)} %bitcast.7) | data formatting | bytes 20480
Async XLA Ops:
  0.0 0.7 %copy-start.5 = (s32[4,64]{1,0:T(4,128)S(1)}, s32[4,64]{1,0:T(4,128)}, u32[]{:S(2)}) copy-start(s32[4,64]{1,0:T(4,128)} %mask_ref.1) | copy-start | bytes 3076
  0.0 0.7 %copy-start.4 = (s32[4,64]{1,0:T(4,128)S(1)}, s32[4,64]{1,0:T(4,128)}, u32[]{:S(2)}) copy-start(s32[4,64]{1,0:T(4,128)} %list_ref.1) | copy-start | bytes 3076
  0.7 1.1 %copy-start = (bf16[80,5120]{1,0:T(8,128)(2,1)S(1)}, bf16[80,5120]{1,0:T(8,128)(2,1)}, u32[]{:S(2)}) copy-start(bf16[80,5120]{1,0:T(8,128)(2,1)} %w_hbm.1) | copy-start | bytes 2457604
  1.8 1.1 %copy-start.1 = (bf16[4,16,5120]{2,1,0:T(8,128)(2,1)S(1)}, bf16[4,16,5120]{2,1,0:T(8,128)(2,1)}, u32[]{:S(2)}) copy-start(bf16[4,16,5120]{2,1,0:T(8,128)(2,1)} %param.6) | copy-start | bytes 1966084
  2.9 1.0 %copy-start.2 = (bf16[2,1,128,1024]{3,2,1,0:T(8,128)(2,1)S(1)}, bf16[2,1,128,1024]{3,2,1,0:T(8,128)(2,1)}, u32[]{:S(2)}) copy-start(bf16[2,1,128,1024]{3,2,1,0:T(8,128)(2,1)} %param.8) | copy-start | bytes 1572868
  4.0 0.9 %copy-start.3 = (bf16[2,4,16,1024]{3,2,1,0:T(8,128)(2,1)S(1)}, bf16[2,4,16,1024]{3,2,1,0:T(8,128)(2,1)}, u32[]{:S(2)}) copy-start(bf16[2,4,16,1024]{3,2,1,0:T(8,128)(2,1)} %param.7) | copy-start | bytes 786436

commit v2 on v1

v2 whole, which is shorter than its diff:
```python
import functools
import math

import jax
import jax.numpy as jnp
from jax import lax
from jax.experimental import pallas as pl
from jax.experimental.pallas import tpu as pltpu
from jax.sharding import PartitionSpec as P

MESH = pl.DeviceIdType.MESH
BF, F32 = jnp.bfloat16, jnp.float32
HIDDEN = -1e30
FLOOR = -1e29


def device(h, m, y, z, c):
    return (h * 2 + c, (y * 8 + z) * 2 + (m + h) % 2)


def kernel(
    q_hbm, f_hbm, kv_hbm, list_hbm, mask_hbm, w_hbm, out_ref,
    list_ref, mask_ref, qb, qc, kvb, fb, eb, bias, m_ref, l_ref, acc, wv, wp, wb,
    msg, accr, attp, att_g, os, orv,
    loc, pg_s, pg_r, fw_s, fw_r, q_s, q_r, w_s, w_r, wx_s, wx_r, wf_s, wf_r,
    ac_s, ac_r, at_s, at_r, o_s, o_r,
):
    g = lax.axis_index("group")
    s = lax.axis_index("shard")
    h, c = g // 2, g % 2
    y, z, l = s // 16, (s // 2) % 8, s % 2
    m = (l + h) % 2
    head = 2 * y + m
    plane = [(0, 0), (1, 0), (0, 1), (0, 3), (1, 1), (1, 3), (0, 2), (1, 2)]
    column = [(dh, dz) for dh in range(2) for dz in range(8)]
    sibling = device(h, m, y, z, 1 - c)
    across = device(1 - h, m, y, z, c)

    def in_plane(j):
        dm, dy = plane[j]
        return device(h, (m + dm) % 2, (y + dy) % 4, z, c)

    def in_column(k):
        dh, dz = column[k]
        return device((h + dh) % 2, m, y, (z + dz) % 8, c)

    holder = z // 4 == m
    w_to = [2 * k + (z + c) % 2 for k in range(4)]
    w_from = [4 * m + 2 * k + (z + c) % 2 for k in range(2)]

    def w_rows(zz, ll):
        return pl.ds(pl.multiple_of(80 * ((zz % 4) * 2 + ll), 16), 80)

    bar = pltpu.get_barrier_semaphore()

    def greet(d):
        pl.semaphore_signal(bar, inc=1, device_id=d, device_id_type=MESH)

    greet(sibling)
    for j in range(1, 8):
        greet(in_plane(j))
    for k in range(1, 16):
        greet(in_column(k))

    cols = pl.ds(pl.multiple_of(head * 128, 128), 128)
    q_cols = pl.ds(pl.multiple_of(head * 640, 128), 640)
    ld_q = pltpu.make_async_copy(q_hbm.at[:, q_cols], qb.at[0], loc.at[0])
    ld_kv = pltpu.make_async_copy(kv_hbm.at[:, :, cols], kvb.at[:, 0], loc.at[1])
    ld_f = pltpu.make_async_copy(f_hbm.at[:, :, cols], fb, loc.at[2])
    ld_w = pltpu.make_async_copy(w_hbm, wv, loc.at[3])
    ld_list = pltpu.make_async_copy(list_hbm, list_ref, loc.at[5])
    ld_mask = pltpu.make_async_copy(mask_hbm, mask_ref, loc.at[6])
    for ld in (ld_list, ld_mask, ld_q, ld_kv, ld_w, ld_f):
        ld.start()

    eb[0] = jnp.full((8, 128), -1, jnp.int32)
    ld_list.wait()
    ld_mask.wait()
    eb[0, 0:4, 0:64] = jnp.where(mask_ref[...] > 0, list_ref[...], -1)

    ld_w.wait()
    for z2 in range(8):
        wp[z2] = jnp.concatenate(
            [wv[:, 1280 * y2 + 160 * z2 : 1280 * y2 + 160 * z2 + 160] for y2 in range(4)], axis=1
        )

    pl.semaphore_wait(bar, 23)

    def send(src, dst, ss, rs, d):
        cp = pltpu.make_async_remote_copy(
            src_ref=src, dst_ref=dst, send_sem=ss, recv_sem=rs, device_id=d, device_id_type=MESH
        )
        cp.start()
        pending.append(cp)
        return cp

    pending = []
    snd_e = send(eb.at[0], eb.at[1], q_s.at[0], q_r.at[0], across)
    pages = [None] * 8
    for j in range(1, 8):
        dm, dy = plane[j]
        there = 2 * ((y + dy) % 4) + (m + dm) % 2
        there_cols = pl.ds(pl.multiple_of(there * 128, 128), 128)
        pages[j] = send(kv_hbm.at[:, :, there_cols], kvb.at[:, j], pg_s.at[j], pg_r.at[j], in_plane(j))
    ld_q.wait()
    snd_q = send(qb.at[0], qb.at[1], q_s.at[1], q_r.at[1], across)
    ld_kv.wait()

    forwards = [None] * 8
    forwards[0] = send(kvb.at[:, 0], kvb.at[:, 8], fw_s.at[0], fw_r.at[0], sibling)

    def w_send(k, slot):
        return pltpu.make_async_remote_copy(
            src_ref=wp.at[w_to[k]], dst_ref=wb.at[w_rows(z, l)], send_sem=w_s.at[k], recv_sem=w_r.at[slot],
            device_id=device(h, m, y, w_to[k], c), device_id_type=MESH,
        )

    def w_keep():
        return pltpu.make_async_copy(wp.at[z], wb.at[w_rows(z, l)], loc.at[4])

    for k in range(4):
        pl.when(holder & (w_to[k] != z))(lambda: w_send(k, (z % 4) // 2).start())
    pl.when(holder & (c == 0))(lambda: w_keep().start())

    def pass_weights_on():
        for k in range(2):
            mine = w_from[k] == z
            pl.when(mine)(lambda: w_keep().wait())
            pl.when(jnp.logical_not(mine))(lambda: w_send(k, k).wait_recv())
            rows = wb.at[w_rows(w_from[k], l)]
            w_cross.append(send(rows, rows, wx_s.at[k], wx_r.at[k], across))
            w_fwd.append(send(rows, rows, wf_s.at[k], wf_r.at[k], sibling))

    def pass_crossed_weights_on():
        for k in range(2):
            w_cross[k].wait_recv()
            rows = wb.at[w_rows(w_from[k], 1 - l)]
            w_fwd.append(send(rows, rows, wf_s.at[2 + k], wf_r.at[2 + k], sibling))

    w_cross, w_fwd = [], []

    def finish():
        for cp in pending:
            cp.wait_send()
        for k in range(4):
            pl.when(holder & (w_to[k] != z))(lambda: w_send(k, 0).wait_send())

    snd_e.wait_recv()
    lists = eb[...].reshape(16, 128)
    row = lax.broadcasted_iota(jnp.int32, (16, 640), 0)
    col = lax.broadcasted_iota(jnp.int32, (16, 640), 1)
    owner = jnp.where(col >= 320, 8, 0) + ((col >> 4) & 3)
    pick = (row == owner).astype(F32)
    for j in range(16):
        dm, dy = plane[j % 8]
        src_m, src_y, src_c = (m - dm + 2) % 2, (y - dy + 4) % 4, (c + j // 8) % 2
        src_l = (src_m + h) % 2
        number = (h * 2 + src_c) * 64 + (src_y * 8 + z) * 2 + src_l
        seen = jnp.max((lists == number).astype(F32), axis=1, keepdims=True)
        bias[pl.ds(j, 1), :] = (jnp.sum(pick * seen, axis=0, keepdims=True) - 1.0) * (-HIDDEN)

    snd_q.wait_recv()
    for o in range(2):
        for i in range(5):
            qc[o * 320 + i * 64 : o * 320 + i * 64 + 64, :] = qb[o, :, i * 128 : i * 128 + 128]

    scale = math.log2(math.e) / math.sqrt(128)

    def scores(keys):
        return lax.dot_general(keys, qc[...], (((1,), (1,)), ((), ())), preferred_element_type=F32) * scale

    def weigh(values, weights):
        return lax.dot_general(
            values, weights.astype(BF), (((0,), (0,)), ((), ())), preferred_element_type=F32
        )

    ld_f.wait()
    key = lax.broadcasted_iota(jnp.int32, (64, 640), 0)
    col = lax.broadcasted_iota(jnp.int32, (64, 640), 1)
    visible = (col < 320) & ((key >> 4) == ((col >> 4) & 3)) & ((key & 15) <= (col & 15)) & (z == 0)
    sc = jnp.where(visible, scores(fb[0]), HIDDEN)
    top = jnp.maximum(jnp.max(sc, axis=0, keepdims=True), FLOOR)
    wt = jnp.exp2(sc - top)
    m_ref[...] = top
    l_ref[...] = jnp.sum(wt, axis=0, keepdims=True)
    acc[...] = weigh(fb[1], wt)

    def block(first):
        sc = scores(kvb[0, first : first + 4].reshape(512, 128))
        sc = (sc.reshape(4, 128, 640) + bias[first : first + 4, :][:, None, :]).reshape(512, 640)
        old = m_ref[...]
        top = jnp.maximum(old, jnp.max(sc, axis=0, keepdims=True))
        keep = jnp.exp2(old - top)
        wt = jnp.exp2(sc - top)
        m_ref[...] = top
        l_ref[...] = l_ref[...] * keep + jnp.sum(wt, axis=0, keepdims=True)
        acc[...] = acc[...] * keep + weigh(kvb[1, first : first + 4].reshape(512, 128), wt)

    def pass_on(j):
        pages[j].wait_recv()
        forwards[j] = send(kvb.at[:, j], kvb.at[:, 8 + j], fw_s.at[j], fw_r.at[j], sibling)

    for j in range(1, 4):
        pass_on(j)
    block(0)
    for j in range(4):
        forwards[j].wait_recv()
    block(8)
    for j in range(4, 8):
        pass_on(j)
    block(4)
    for j in range(4, 8):
        forwards[j].wait_recv()
    block(12)

    def pieces(x, n):
        out = []
        for _ in range(n):
            out.append(x.astype(BF).astype(F32))
            x = x - out[-1]
        return out

    sums_rows = acc[...].T
    stats = jnp.concatenate(
        pieces(m_ref[...], 3) + pieces(l_ref[...], 2) + [jnp.zeros((3, 640), F32)], axis=0
    )
    for o in range(2):
        for k in range(8):
            at = slice(o * 320 + k * 40, o * 320 + k * 40 + 40)
            tail = jnp.concatenate([stats[:, at], jnp.zeros((8, 88), F32)], axis=1)
            msg[o, k] = jnp.concatenate([sums_rows[at], tail], axis=0).astype(BF)
    parts = [None] * 16
    for k in (12, 4, 11, 13, 3, 5, 10, 14, 2, 6, 9, 15, 1, 7, 8):
        dh, dz = column[k]
        parts[k] = send(msg.at[dh, (z + dz) % 8], accr.at[k], ac_s.at[k], ac_r.at[k], in_column(k))
    accr[0] = msg[0, z]

    pass_weights_on()
    for k in range(1, 16):
        parts[k].wait_recv()
    stats = accr[:, 32:48, :].astype(F32)
    tops = stats[:, 8] + stats[:, 9] + stats[:, 10]
    sums = stats[:, 11] + stats[:, 12]
    factor = jnp.exp2(tops - jnp.max(tops, axis=0, keepdims=True))
    factor = (factor / jnp.sum(factor * sums, axis=0, keepdims=True)).T
    total = jnp.zeros((48, 128), F32)
    for k in range(16):
        total = total + accr[k].astype(F32) * factor[0:48, k : k + 1]
    attp[...] = total.astype(BF)

    gathered = [None] * 8
    for dz in (4, 3, 5, 2, 6, 1, 7):
        gathered[dz] = send(attp, att_g.at[z], at_s.at[dz], at_r.at[dz], in_column(dz))
    att_g[z] = attp[...]
    pass_crossed_weights_on()
    for k in range(4):
        w_fwd[k].wait_recv()
    for dz in range(1, 8):
        gathered[dz].wait_recv()

    att = att_g[...].astype(F32)[:, :40].reshape(320, 128).astype(BF)
    proj = jnp.zeros((64, 640), F32)
    for i in range(5):
        proj += jnp.dot(att[i * 64 : i * 64 + 64], wb[i * 128 : i * 128 + 128, :], preferred_element_type=F32)
    for k in range(8):
        os[k] = jnp.concatenate([proj[:, 80 * k : 80 * k + 80], jnp.zeros((64, 48), F32)], axis=1).astype(BF)
    outs = [None] * 8
    for j in (7, 6, 5, 4, 3, 2, 1):
        dm, dy = plane[j]
        k = 2 * ((y + dy) % 4) + ((m + dm) % 2 + h) % 2
        outs[j] = send(os.at[k], orv.at[j], o_s.at[j], o_r.at[j], in_plane(j))
    result = os[2 * y + l].astype(F32)
    for j in range(1, 8):
        outs[j].wait_recv()
        result += orv[j].astype(F32)
    out_ref[...] = result[:, :80].astype(BF)

    finish()


def on_device(queries, fresh_kv, kv_pages, page_list, tile_mask, out_weight):
    hbm, vmem = pl.BlockSpec(memory_space=pltpu.HBM), pl.BlockSpec(memory_space=pltpu.VMEM)
    sem = lambda n: pltpu.SemaphoreType.DMA((n,))
    out = pl.pallas_call(
        kernel,
        out_shape=jax.ShapeDtypeStruct((64, 80), BF),
        in_specs=[hbm] * 6,
        out_specs=vmem,
        scratch_shapes=[
            pltpu.VMEM((4, 64), jnp.int32),
            pltpu.VMEM((4, 64), jnp.int32),
            pltpu.VMEM((2, 64, 640), BF),
            pltpu.VMEM((640, 128), BF),
            pltpu.VMEM((2, 16, 128, 128), BF),
            pltpu.VMEM((2, 64, 128), BF),
            pltpu.VMEM((2, 8, 128), jnp.int32),
            pltpu.VMEM((16, 640), F32),
            pltpu.VMEM((1, 640), F32),
            pltpu.VMEM((1, 640), F32),
            pltpu.VMEM((128, 640), F32),
            pltpu.VMEM((80, 5120), BF),
            pltpu.VMEM((8, 80, 640), BF),
            pltpu.VMEM((640, 640), BF),
            pltpu.VMEM((2, 8, 48, 128), BF),
            pltpu.VMEM((16, 48, 128), BF),
            pltpu.VMEM((48, 128), BF),
            pltpu.VMEM((8, 48, 128), BF),
            pltpu.VMEM((8, 64, 128), BF),
            pltpu.VMEM((8, 64, 128), BF),
            sem(7), sem(8), sem(8), sem(8), sem(8), sem(2), sem(2), sem(4), sem(2), sem(2), sem(2), sem(4), sem(4),
            sem(16), sem(16), sem(8), sem(8), sem(8), sem(8),
        ],
        compiler_params=pltpu.CompilerParams(
            collective_id=0, has_side_effects=True, vmem_limit_bytes=62 * 2**20
        ),
        name="attend",
    )(
        queries.reshape(64, 5120),
        fresh_kv.reshape(2, 64, 1024),
        kv_pages.reshape(2, 128, 1024),
        page_list,
        tile_mask,
        out_weight,
    )
    return out.reshape(4, 16, 80)


def solution(mesh):
    return jax.shard_map(
        on_device,
        mesh=mesh,
        in_specs=(
            P("group", None, None),
            P(None, "group", None, None),
            P(None, ("group", "shard"), None, None),
            P("group", None),
            P("group", None),
            P("shard", None),
        ),
        out_specs=P("group", None, "shard"),
        check_vma=False,
    )
```

time: 48.4 us -> 41.2 us (0.85); the launches traced: 47.7 us -> 41 us
  local copies, waits for them, and re-layouts: 5.53 us -> 1.32 us
  Pallas kernels: 42.1 us -> 39.6 us
    unnamed x13 -> x1, local copies, waits for them, and re-layouts: 5.53 us -> 1.32 us
    pallas_call x1, Pallas kernels: 42.1 us -> 39.6 us  [on_device(): pl.pallas_call(kernel, out_shape=jax.ShapeDtypeStruct((64, 80), BF), in_s...]
where the time goes in v2:
time: 41.2 us; the launch traced here: 41 us
  Pallas kernels  39.6 us (96%)
  local copies, waits for them, and re-layouts  1.32 us (3%)
    pallas_call x1, Pallas kernels, on_device(): pl.pallas_call(kernel, out_shape=jax.ShapeDtypeStruct((64, 80), BF), in_s...  39.6 us
    unnamed x1, local copies, waits for them, and re-layouts  1.32 us

profile of v2, /device:TPU:4, one launch (start us, length us, event | category | flops | bytes accessed | tf_op | source)
XLA Modules:
  0.0 41.0 jit_solution(14277712521519332271)
XLA Ops:
  0.0 39.6 %attend.1 = bf16[64,80]{1,0:T(8,128)(2,1)} custom-call(bf16[64,5120]{1,0:T(8,128)(2,1)} %bitcast.4, bf16[2,64,1024]{2,1,0:T(8,128)(2,1)} %bitcast.6, bf16[2,128,1024]{2,1,0:T(8,128)(2,1)} %bitcast.5, s32[4,64]{1,0:T(4,128)} %list_hbm.1, s32[4,64]{1,0:T(4,128)} %mask_hbm.1, bf16[80,5120]{1,0:T(8,128)(2,1)} %w_hbm.1), custom_call_target="tpu_custom_call" | custom-call | tf_op jit(solution)/shard_map/attend/pallas_call | solution.py:284
  39.6 1.3 %copy.8 = bf16[4,16,80]{2,1,0:T(8,128)(2,1)} copy(bf16[4,16,80]{2,1,0:T(8,128)(2,1)} %bitcast.7) | data formatting | bytes 20480

commit v3 on v2

v3 whole, which is shorter than its diff:
```python
import functools
import math

import jax
import jax.numpy as jnp
from jax import lax
from jax.experimental import pallas as pl
from jax.experimental.pallas import tpu as pltpu
from jax.sharding import PartitionSpec as P

MESH = pl.DeviceIdType.MESH
BF, F32 = jnp.bfloat16, jnp.float32
HIDDEN = -1e30
FLOOR = -1e29
FAR_FIRST = (12, 4, 11, 13, 3, 5, 10, 14, 2, 6, 9, 15, 1, 7, 8)


def device(h, m, y, z, c):
    return (h * 2 + c, (y * 8 + z) * 2 + (m + h) % 2)


def kernel(
    q_hbm, f_hbm, kv_hbm, list_hbm, mask_hbm, w_hbm, out_ref,
    list_ref, mask_ref, qb, qc, kvb, fb, eb, bias, m_ref, l_ref, acc, wv, wp, wb,
    msg, accr, attp, att_g, os, orv,
    loc, pg_s, pg_r, fw_s, fw_r, q_s, q_r, w_s, w_r, wx_s, wx_r,
    ac_s, ac_r, at_s, at_r, o_s, o_r,
):
    g = lax.axis_index("group")
    s = lax.axis_index("shard")
    h, c = g // 2, g % 2
    y, z, l = s // 16, (s // 2) % 8, s % 2
    m = (l + h) % 2
    head = 2 * y + m
    plane = [(0, 0), (1, 0), (0, 1), (0, 3), (1, 1), (1, 3), (0, 2), (1, 2)]
    column = [(dh, dz) for dh in range(2) for dz in range(8)]
    sibling = device(h, m, y, z, 1 - c)
    across = device(1 - h, m, y, z, c)

    def in_plane(j, core):
        dm, dy = plane[j]
        return device(h, (m + dm) % 2, (y + dy) % 4, z, core)

    def in_column(k, core):
        dh, dz = column[k]
        return device((h + dh) % 2, m, y, (z + dz) % 8, core)

    holder = z // 4 == m
    w_to = [2 * k + (z + c) % 2 for k in range(4)]

    def w_rows(zz, ll):
        return pl.ds(pl.multiple_of(80 * ((zz % 4) * 2 + ll), 16), 80)

    bar = pltpu.get_barrier_semaphore()

    def greet(d):
        pl.semaphore_signal(bar, inc=1, device_id=d, device_id_type=MESH)

    @pl.when(c == 1)
    def _():
        for k in FAR_FIRST:
            greet(in_column(k, 1))
            greet(in_column(k, 0))
        for j in range(7, 0, -1):
            greet(in_plane(j, 1))

    for j in range(7, 0, -1):
        greet(in_plane(j, 1 - c))
    greet(sibling)
    pl.when(c == 0)(lambda: greet(across))

    cols = pl.ds(pl.multiple_of(head * 128, 128), 128)
    q_cols = pl.ds(pl.multiple_of(head * 640, 128), 640)
    ld_q = pltpu.make_async_copy(q_hbm.at[:, q_cols], qb.at[0], loc.at[0])
    ld_kv = pltpu.make_async_copy(kv_hbm.at[:, :, cols], kvb.at[:, 0], loc.at[1])
    ld_f = pltpu.make_async_copy(f_hbm.at[:, :, cols], fb, loc.at[2])
    ld_w = pltpu.make_async_copy(w_hbm, wv, loc.at[3])
    ld_list = pltpu.make_async_copy(list_hbm, list_ref, loc.at[5])
    ld_mask = pltpu.make_async_copy(mask_hbm, mask_ref, loc.at[6])
    for ld in (ld_list, ld_mask, ld_q, ld_kv, ld_w, ld_f):
        ld.start()

    eb[0] = jnp.full((8, 128), -1, jnp.int32)
    ld_list.wait()
    ld_mask.wait()
    eb[0, 0:4, 0:64] = jnp.where(mask_ref[...] > 0, list_ref[...], -1)

    ld_w.wait()
    for z2 in range(8):
        wp[z2] = jnp.concatenate(
            [wv[:, 1280 * y2 + 160 * z2 : 1280 * y2 + 160 * z2 + 160] for y2 in range(4)], axis=1
        )

    pl.semaphore_wait(bar, 24 + 6 * c)

    def send(src, dst, ss, rs, d):
        cp = pltpu.make_async_remote_copy(
            src_ref=src, dst_ref=dst, send_sem=ss, recv_sem=rs, device_id=d, device_id_type=MESH
        )
        cp.start()
        pending.append(cp)
        return cp

    def forward(j):
        return pltpu.make_async_remote_copy(
            src_ref=kvb.at[:, j], dst_ref=kvb.at[:, 8 + j], send_sem=fw_s.at[j], recv_sem=fw_r.at[j],
            device_id=sibling, device_id_type=MESH,
        )

    def pages_in(j):
        return pltpu.make_async_remote_copy(
            src_ref=kvb.at[:, 0], dst_ref=kvb.at[:, j], send_sem=pg_s.at[j], recv_sem=pg_r.at[j],
            device_id=sibling, device_id_type=MESH,
        )

    pending = []
    snd_e = send(eb.at[0], eb.at[1], q_s.at[0], q_r.at[0], across)
    for j in range(1, 8):
        dm, dy = plane[j]
        there = 2 * ((y + dy) % 4) + (m + dm) % 2
        there_cols = pl.ds(pl.multiple_of(there * 128, 128), 128)
        send(kv_hbm.at[:, :, there_cols], kvb.at[:, j], pg_s.at[j], pg_r.at[j], in_plane(j, 1 - c))
    ld_q.wait()
    snd_q = send(qb.at[0], qb.at[1], q_s.at[1], q_r.at[1], across)
    ld_kv.wait()

    forward(0).start()

    def w_send(k):
        return pltpu.make_async_remote_copy(
            src_ref=wp.at[w_to[k]], dst_ref=wb.at[w_rows(z, l)], send_sem=w_s.at[k], recv_sem=w_r.at[z % 4],
            device_id=device(h, m, y, w_to[k], 1), device_id_type=MESH,
        )

    def w_cross(k):
        rows = wb.at[w_rows(k, l)]
        return pltpu.make_async_remote_copy(
            src_ref=rows, dst_ref=rows, send_sem=wx_s.at[k], recv_sem=wx_r.at[k], device_id=across, device_id_type=MESH
        )

    for k in range(4):
        pl.when(holder)(lambda: w_send(k).start())

    def w_pass_on(k):
        pltpu.make_async_remote_copy(
            src_ref=wp.at[0], dst_ref=wb.at[w_rows(k, l)], send_sem=w_s.at[k], recv_sem=w_r.at[k],
            device_id=across, device_id_type=MESH,
        ).wait_recv()
        w_cross(k).start()

    snd_e.wait_recv()
    lists = eb[...].reshape(16, 128)
    row = lax.broadcasted_iota(jnp.int32, (16, 640), 0)
    col = lax.broadcasted_iota(jnp.int32, (16, 640), 1)
    owner = jnp.where(col >= 320, 8, 0) + ((col >> 4) & 3)
    pick = (row == owner).astype(F32)
    for j in range(16):
        dm, dy = plane[j % 8]
        src_m, src_y, src_c = (m - dm + 2) % 2, (y - dy + 4) % 4, (c + j // 8 + min(j % 8, 1)) % 2
        src_l = (src_m + h) % 2
        number = (h * 2 + src_c) * 64 + (src_y * 8 + z) * 2 + src_l
        seen = jnp.max((lists == number).astype(F32), axis=1, keepdims=True)
        bias[j] = (jnp.sum(pick * seen, axis=0, keepdims=True) - 1.0) * (-HIDDEN)

    snd_q.wait_recv()
    for o in range(2):
        for i in range(5):
            qc[o * 320 + i * 64 : o * 320 + i * 64 + 64, :] = qb[o, :, i * 128 : i * 128 + 128]

    scale = math.log2(math.e) / math.sqrt(128)

    def scores(keys):
        return lax.dot_general(keys, qc[...], (((1,), (1,)), ((), ())), preferred_element_type=F32) * scale

    def weigh(values, weights):
        return lax.dot_general(
            values, weights.astype(BF), (((0,), (0,)), ((), ())), preferred_element_type=F32
        )

    ld_f.wait()
    key = lax.broadcasted_iota(jnp.int32, (64, 640), 0)
    col = lax.broadcasted_iota(jnp.int32, (64, 640), 1)
    visible = (col < 320) & ((key >> 4) == ((col >> 4) & 3)) & ((key & 15) <= (col & 15)) & (z == 0)
    sc = jnp.where(visible, scores(fb[0]), HIDDEN)
    top = jnp.maximum(jnp.max(sc, axis=0, keepdims=True), FLOOR)
    wt = jnp.exp2(sc - top)
    m_ref[...] = top
    l_ref[...] = jnp.sum(wt, axis=0, keepdims=True)
    acc[...] = weigh(fb[1], wt)

    @pl.loop(0, 4)
    def _(n):
        @pl.when(n % 2 == 0)
        def _():
            for j in range(4):
                @pl.when(n + j > 0)
                def _():
                    pages_in(2 * n + j).wait_recv()
                    forward(2 * n + j).start()

        @pl.when(n % 2 == 1)
        def _():
            for j in range(4):
                forward(2 * (n - 1) + j).wait_recv()

        first = (n % 2) * 8 + (n // 2) * 4
        slots = pl.ds(first, 4)
        sc = scores(kvb[0, slots].reshape(512, 128))
        sc = (sc.reshape(4, 128, 640) + bias[slots]).reshape(512, 640)
        old = m_ref[...]
        top = jnp.maximum(old, jnp.max(sc, axis=0, keepdims=True))
        keep = jnp.exp2(old - top)
        wt = jnp.exp2(sc - top)
        m_ref[...] = top
        l_ref[...] = l_ref[...] * keep + jnp.sum(wt, axis=0, keepdims=True)
        acc[...] = acc[...] * keep + weigh(kvb[1, slots].reshape(512, 128), wt)

    def pieces(x, n):
        out = []
        for _ in range(n):
            out.append(x.astype(BF).astype(F32))
            x = x - out[-1]
        return out

    sums_rows = acc[...].T
    stats = jnp.concatenate(
        pieces(m_ref[...], 3) + pieces(l_ref[...], 2) + [jnp.zeros((3, 640), F32)], axis=0
    )
    for o in range(2):
        for k in range(8):
            at = slice(o * 320 + k * 40, o * 320 + k * 40 + 40)
            tail = jnp.concatenate([stats[:, at], jnp.zeros((8, 88), F32)], axis=1)
            msg[o, k] = jnp.concatenate([sums_rows[at], tail], axis=0).astype(BF)
    def part(k):
        dh, dz = column[k]
        return pltpu.make_async_remote_copy(
            src_ref=msg.at[dh, (z + dz) % 8], dst_ref=accr.at[c * 16 + k], send_sem=ac_s.at[k], recv_sem=ac_r.at[c * 16 + k],
            device_id=in_column(k, 1), device_id_type=MESH,
        )

    def part_in(i):
        return pltpu.make_async_remote_copy(
            src_ref=msg.at[0, 0], dst_ref=accr.at[i], send_sem=ac_s.at[0], recv_sem=ac_r.at[i],
            device_id=sibling, device_id_type=MESH,
        )

    def piece_to(dz):
        return pltpu.make_async_remote_copy(
            src_ref=attp, dst_ref=att_g.at[z], send_sem=at_s.at[dz], recv_sem=at_r.at[dz],
            device_id=in_column(dz, 1), device_id_type=MESH,
        )

    def out_to(j, core):
        dm, dy = plane[j]
        k = 2 * ((y + dy) % 4) + ((m + dm) % 2 + h) % 2
        return pltpu.make_async_remote_copy(
            src_ref=os.at[k, core], dst_ref=orv.at[j], send_sem=o_s.at[core * 8 + j], recv_sem=o_r.at[j],
            device_id=in_plane(j, core), device_id_type=MESH,
        )

    for k in FAR_FIRST:
        part(k).start()
    pl.when(c == 0)(lambda: part(0).start())

    @pl.when(c == 1)
    def _():
        accr[16] = msg[0, z]
        for k in range(4):
            w_pass_on(k)
        for i in range(32):
            if i != 16:
                part_in(i).wait_recv()
        for i in range(2):
            ours = slice(16 * i, 16 * i + 16)
            stats = accr[ours, 32:48, :].astype(F32)
            tops = stats[:, 8] + stats[:, 9] + stats[:, 10]
            sums = stats[:, 11] + stats[:, 12]
            factor = jnp.exp2(tops - jnp.max(tops, axis=0, keepdims=True))
            factor = (factor / jnp.sum(factor * sums, axis=0, keepdims=True)).T
            total = jnp.zeros((48, 128), F32)
            for k in range(16):
                total = total + accr[16 * i + k].astype(F32) * factor[0:48, k : k + 1]
            attp[i] = total.astype(BF)
        for dz in (4, 3, 5, 2, 6, 1, 7):
            piece_to(dz).start()
        att_g[z] = attp[...]
        for k in range(4):
            pltpu.make_async_remote_copy(
                src_ref=wp.at[0], dst_ref=wb.at[w_rows(k, 1 - l)], send_sem=wx_s.at[k], recv_sem=wx_r.at[k],
                device_id=across, device_id_type=MESH,
            ).wait_recv()
        for dz in range(1, 8):
            pltpu.make_async_remote_copy(
                src_ref=attp, dst_ref=att_g.at[(z - dz + 8) % 8], send_sem=at_s.at[dz], recv_sem=at_r.at[dz],
                device_id=sibling, device_id_type=MESH,
            ).wait_recv()
        att = [att_g[:, i].astype(F32)[:, :40].reshape(320, 128).astype(BF) for i in range(2)]
        proj = jnp.zeros((128, 640), F32)
        for i in range(5):
            rows = slice(i * 64, i * 64 + 64)
            proj += jnp.dot(
                jnp.concatenate([att[0][rows], att[1][rows]], axis=0), wb[i * 128 : i * 128 + 128, :],
                preferred_element_type=F32,
            )
        for k in range(8):
            chunk = jnp.concatenate([proj[:, 80 * k : 80 * k + 80], jnp.zeros((128, 48), F32)], axis=1)
            os[k] = chunk.astype(BF).reshape(2, 64, 128)
        for j in range(7, -1, -1):
            out_to(j, 0).start()
            if j:
                out_to(j, 1).start()
        orv[0] = os[2 * y + l, 1]

    result = jnp.zeros((64, 128), F32)
    pl.when(c == 0)(lambda: out_to(0, 0).wait_recv())
    for j in range(7, -1, -1):
        if j:
            out_to(j, 0).wait_recv()
        result += orv[j].astype(F32)
    out_ref[...] = result[:, :80].astype(BF)

    for cp in pending:
        cp.wait_send()
    for j in range(8):
        forward(j).wait_send()
    for k in range(4):
        pl.when(holder)(lambda: w_send(k).wait_send())
    for k in FAR_FIRST:
        part(k).wait_send()
    pl.when(c == 0)(lambda: part(0).wait_send())

    @pl.when(c == 1)
    def _():
        for k in range(4):
            w_cross(k).wait_send()
        for dz in range(1, 8):
            piece_to(dz).wait_send()
        for j in range(8):
            out_to(j, 0).wait_send()
            if j:
                out_to(j, 1).wait_send()


def on_device(queries, fresh_kv, kv_pages, page_list, tile_mask, out_weight):
    hbm, vmem = pl.BlockSpec(memory_space=pltpu.HBM), pl.BlockSpec(memory_space=pltpu.VMEM)
    sem = lambda n: pltpu.SemaphoreType.DMA((n,))
    out = pl.pallas_call(
        kernel,
        out_shape=jax.ShapeDtypeStruct((64, 80), BF),
        in_specs=[hbm] * 6,
        out_specs=vmem,
        scratch_shapes=[
            pltpu.VMEM((4, 64), jnp.int32),
            pltpu.VMEM((4, 64), jnp.int32),
            pltpu.VMEM((2, 64, 640), BF),
            pltpu.VMEM((640, 128), BF),
            pltpu.VMEM((2, 16, 128, 128), BF),
            pltpu.VMEM((2, 64, 128), BF),
            pltpu.VMEM((2, 8, 128), jnp.int32),
            pltpu.VMEM((16, 1, 640), F32),
            pltpu.VMEM((1, 640), F32),
            pltpu.VMEM((1, 640), F32),
            pltpu.VMEM((128, 640), F32),
            pltpu.VMEM((80, 5120), BF),
            pltpu.VMEM((8, 80, 640), BF),
            pltpu.VMEM((640, 640), BF),
            pltpu.VMEM((2, 8, 48, 128), BF),
            pltpu.VMEM((32, 48, 128), BF),
            pltpu.VMEM((2, 48, 128), BF),
            pltpu.VMEM((8, 2, 48, 128), BF),
            pltpu.VMEM((8, 2, 64, 128), BF),
            pltpu.VMEM((8, 64, 128), BF),
            sem(7), sem(8), sem(8), sem(8), sem(8), sem(2), sem(2), sem(4), sem(4), sem(4), sem(4),
            sem(16), sem(32), sem(8), sem(8), sem(16), sem(8),
        ],
        compiler_params=pltpu.CompilerParams(
            collective_id=0, has_side_effects=True, vmem_limit_bytes=int(53.9 * 2**20)
        ),
        name="attend",
    )(
        queries.reshape(64, 5120),
        fresh_kv.reshape(2, 64, 1024),
        kv_pages.reshape(2, 128, 1024),
        page_list,
        tile_mask,
        out_weight,
    )
    return out.reshape(4, 16, 80)


def solution(mesh):
    return jax.shard_map(
        on_device,
        mesh=mesh,
        in_specs=(
            P("group", None, None),
            P(None, "group", None, None),
            P(None, ("group", "shard"), None, None),
            P("group", None),
            P("group", None),
            P("shard", None),
        ),
        out_specs=P("group", None, "shard"),
        check_vma=False,
    )
```

time: 41.2 us -> 40.4 us (0.981)
  the two profiles are of different devices: /device:TPU:4 before, /device:TPU:1 now
where the time goes in v3:
time: 40.4 us; the launch traced here: 40.3 us
  Pallas kernels  39 us (97%)
  local copies, waits for them, and re-layouts  1.3 us (3%)
    pallas_call x1, Pallas kernels, on_device(): pl.pallas_call(kernel, out_shape=jax.ShapeDtypeStruct((64, 80), BF), in_s...  39 us
    unnamed x5, local copies, waits for them, and re-layouts  1.3 us

profile of v3, /device:TPU:1, one launch (start us, length us, event | category | flops | bytes accessed | tf_op | source)
XLA Modules:
  0.0 40.3 jit_solution(11400085042846813106)
XLA Ops:
  0.0 0.0 copy-start.1
  0.0 0.0 copy-start
  0.0 0.7 %copy-done.1 = s32[4,64]{1,0:T(4,128)S(1)} copy-done((s32[4,64]{1,0:T(4,128)S(1)}, s32[4,64]{1,0:T(4,128)}, u32[]{:S(2)}) %copy-start.1) | copy-done | bytes 1048
  0.7 0.0 copy-done
  0.7 39.0 %attend.1 = bf16[64,80]{1,0:T(8,128)(2,1)S(1)} custom-call(bf16[64,5120]{1,0:T(8,128)(2,1)} %bitcast.5, bf16[2,64,1024]{2,1,0:T(8,128)(2,1)} %bitcast.7, bf16[2,128,1024]{2,1,0:T(8,128)(2,1)} %bitcast.6, s32[4,64]{1,0:T(4,128)S(1)} %copy-done, s32[4,64]{1,0:T(4,128)S(1)} %copy-done.1, bf16[80,5120]{1,0:T(8,128)(2,1)} %w_hbm.1), custom_call_target="tpu_custom_call" | custom-call | tf_op jit(solution)/shard_map/attend/pallas_call | solution.py:347
  39.7 0.6 %copy.8 = bf16[4,16,80]{2,1,0:T(8,128)(2,1)} copy(bf16[4,16,80]{2,1,0:T(8,128)(2,1)S(1)} %bitcast.4) | data formatting | bytes 20480
Async XLA Ops:
  0.0 0.7 %copy-start.1 = (s32[4,64]{1,0:T(4,128)S(1)}, s32[4,64]{1,0:T(4,128)}, u32[]{:S(2)}) copy-start(s32[4,64]{1,0:T(4,128)} %mask_hbm.1) | copy-start | bytes 3076
  0.0 0.7 %copy-start = (s32[4,64]{1,0:T(4,128)S(1)}, s32[4,64]{1,0:T(4,128)}, u32[]{:S(2)}) copy-start(s32[4,64]{1,0:T(4,128)} %list_hbm.1) | copy-start | bytes 3076

commit v4 on v3

--- a/solution.py
+++ b/solution.py
@@ -80,17 +80,6 @@
     for ld in (ld_list, ld_mask, ld_q, ld_kv, ld_w, ld_f):
         ld.start()
 
-    eb[0] = jnp.full((8, 128), -1, jnp.int32)
-    ld_list.wait()
-    ld_mask.wait()
-    eb[0, 0:4, 0:64] = jnp.where(mask_ref[...] > 0, list_ref[...], -1)
-
-    ld_w.wait()
-    for z2 in range(8):
-        wp[z2] = jnp.concatenate(
-            [wv[:, 1280 * y2 + 160 * z2 : 1280 * y2 + 160 * z2 + 160] for y2 in range(4)], axis=1
-        )
-
     pl.semaphore_wait(bar, 24 + 6 * c)
 
     def send(src, dst, ss, rs, d):
@@ -114,17 +103,27 @@
         )
 
     pending = []
-    snd_e = send(eb.at[0], eb.at[1], q_s.at[0], q_r.at[0], across)
     for j in range(1, 8):
         dm, dy = plane[j]
         there = 2 * ((y + dy) % 4) + (m + dm) % 2
         there_cols = pl.ds(pl.multiple_of(there * 128, 128), 128)
         send(kv_hbm.at[:, :, there_cols], kvb.at[:, j], pg_s.at[j], pg_r.at[j], in_plane(j, 1 - c))
+    eb[0] = jnp.full((8, 128), -1, jnp.int32)
+    ld_list.wait()
+    ld_mask.wait()
+    eb[0, 0:4, 0:64] = jnp.where(mask_ref[...] > 0, list_ref[...], -1)
+    snd_e = send(eb.at[0], eb.at[1], q_s.at[0], q_r.at[0], across)
     ld_q.wait()
     snd_q = send(qb.at[0], qb.at[1], q_s.at[1], q_r.at[1], across)
     ld_kv.wait()
 
     forward(0).start()
+
+    ld_w.wait()
+    for z2 in range(8):
+        wp[z2] = jnp.concatenate(
+            [wv[:, 1280 * y2 + 160 * z2 : 1280 * y2 + 160 * z2 + 160] for y2 in range(4)], axis=1
+        )
 
     def w_send(k):
         return pltpu.make_async_remote_copy(
@@ -226,16 +225,18 @@
     stats = jnp.concatenate(
         pieces(m_ref[...], 3) + pieces(l_ref[...], 2) + [jnp.zeros((3, 640), F32)], axis=0
     )
-    for o in range(2):
+    def fill(o):
         for k in range(8):
             at = slice(o * 320 + k * 40, o * 320 + k * 40 + 40)
             tail = jnp.concatenate([stats[:, at], jnp.zeros((8, 88), F32)], axis=1)
             msg[o, k] = jnp.concatenate([sums_rows[at], tail], axis=0).astype(BF)
-    def part(k):
-        dh, dz = column[k]
+
+    def part(half, dz):
+        dh = (half + h) % 2
+        k = dh * 8 + dz
         return pltpu.make_async_remote_copy(
             src_ref=msg.at[dh, (z + dz) % 8], dst_ref=accr.at[c * 16 + k], send_sem=ac_s.at[k], recv_sem=ac_r.at[c * 16 + k],
-            device_id=in_column(k, 1), device_id_type=MESH,
+            device_id=device(half, m, y, (z + dz) % 8, 1), device_id_type=MESH,
         )
 
     def part_in(i):
@@ -258,9 +259,12 @@
             device_id=in_plane(j, core), device_id_type=MESH,
         )
 
-    for k in FAR_FIRST:
-        part(k).start()
-    pl.when(c == 0)(lambda: part(0).start())
+    fill(0)
+    fill(1)
+    others = [(half, dz) for dz in (4, 3, 5, 2, 6, 1, 7) for half in range(2)] + [(1 - h, 0)]
+    for half, dz in others:
+        part(half, dz).start()
+    pl.when(c == 0)(lambda: part(h, 0).start())
 
     @pl.when(c == 1)
     def _():
@@ -270,17 +274,16 @@
         for i in range(32):
             if i != 16:
                 part_in(i).wait_recv()
+        stats = accr[:, 32:48, :].astype(F32)
+        tops = (stats[:, 8] + stats[:, 9] + stats[:, 10]).reshape(2, 16, 128)
+        sums = (stats[:, 11] + stats[:, 12]).reshape(2, 16, 128)
+        factor = jnp.exp2(tops - jnp.max(tops, axis=1, keepdims=True))
+        factor = (factor / jnp.sum(factor * sums, axis=1, keepdims=True)).reshape(32, 128).T
         for i in range(2):
-            ours = slice(16 * i, 16 * i + 16)
-            stats = accr[ours, 32:48, :].astype(F32)
-            tops = stats[:, 8] + stats[:, 9] + stats[:, 10]
-            sums = stats[:, 11] + stats[:, 12]
-            factor = jnp.exp2(tops - jnp.max(tops, axis=0, keepdims=True))
-            factor = (factor / jnp.sum(factor * sums, axis=0, keepdims=True)).T
-            total = jnp.zeros((48, 128), F32)
-            for k in range(16):
-                total = total + accr[16 * i + k].astype(F32) * factor[0:48, k : k + 1]
-            attp[i] = total.astype(BF)
+            total = jnp.zeros((40, 128), F32)
+            for k in range(16 * i, 16 * i + 16):
+                total = total + accr[k, 0:40].astype(F32) * factor[0:40, k : k + 1]
+            attp[i] = jnp.concatenate([total, jnp.zeros((8, 128), F32)], axis=0).astype(BF)
         for dz in (4, 3, 5, 2, 6, 1, 7):
             piece_to(dz).start()
         att_g[z] = attp[...]
@@ -302,9 +305,10 @@
                 jnp.concatenate([att[0][rows], att[1][rows]], axis=0), wb[i * 128 : i * 128 + 128, :],
                 preferred_element_type=F32,
             )
+        proj = proj.astype(BF)
         for k in range(8):
-            chunk = jnp.concatenate([proj[:, 80 * k : 80 * k + 80], jnp.zeros((128, 48), F32)], axis=1)
-            os[k] = chunk.astype(BF).reshape(2, 64, 128)
+            for i in range(2):
+                os[k, i, :, 0:80] = proj[64 * i : 64 * i + 64, 80 * k : 80 * k + 80]
         for j in range(7, -1, -1):
             out_to(j, 0).start()
             if j:
@@ -325,9 +329,9 @@
         forward(j).wait_send()
     for k in range(4):
         pl.when(holder)(lambda: w_send(k).wait_send())
-    for k in FAR_FIRST:
-        part(k).wait_send()
-    pl.when(c == 0)(lambda: part(0).wait_send())
+    for half, dz in others:
+        part(half, dz).wait_send()
+    pl.when(c == 0)(lambda: part(h, 0).wait_send())
 
     @pl.when(c == 1)
     def _():

time: 40.4 us -> 40.3 us (level)
  the two profiles are of different devices: /device:TPU:1 before, /device:TPU:4 now
where the time goes in v4:
time: 40.3 us; the launch traced here: 39.8 us
  Pallas kernels  38.5 us (96%)
  local copies, waits for them, and re-layouts  1.3 us (3%)
    pallas_call x1, Pallas kernels, on_device(): pl.pallas_call(kernel, out_shape=jax.ShapeDtypeStruct((64, 80), BF), in_s...  38.5 us
    unnamed x5, local copies, waits for them, and re-layouts  1.3 us

profile of v4, /device:TPU:4, one launch (start us, length us, event | category | flops | bytes accessed | tf_op | source)
XLA Modules:
  0.0 39.8 jit_solution(2712795618234862191)
XLA Ops:
  0.0 0.0 copy-start.1
  0.0 0.0 copy-start
  0.0 0.7 %copy-done.1 = s32[4,64]{1,0:T(4,128)S(1)} copy-done((s32[4,64]{1,0:T(4,128)S(1)}, s32[4,64]{1,0:T(4,128)}, u32[]{:S(2)}) %copy-start.1) | copy-done | bytes 1048
  0.7 0.0 copy-done
  0.7 38.5 %attend.1 = bf16[64,80]{1,0:T(8,128)(2,1)S(1)} custom-call(bf16[64,5120]{1,0:T(8,128)(2,1)} %bitcast.5, bf16[2,64,1024]{2,1,0:T(8,128)(2,1)} %bitcast.7, bf16[2,128,1024]{2,1,0:T(8,128)(2,1)} %bitcast.6, s32[4,64]{1,0:T(4,128)S(1)} %copy-done, s32[4,64]{1,0:T(4,128)S(1)} %copy-done.1, bf16[80,5120]{1,0:T(8,128)(2,1)} %w_hbm.1), custom_call_target="tpu_custom_call" | custom-call | tf_op jit(solution)/shard_map/attend/pallas_call | solution.py:351
  39.2 0.6 %copy.8 = bf16[4,16,80]{2,1,0:T(8,128)(2,1)} copy(bf16[4,16,80]{2,1,0:T(8,128)(2,1)S(1)} %bitcast.4) | data formatting | bytes 20480
Async XLA Ops:
  0.0 0.7 %copy-start.1 = (s32[4,64]{1,0:T(4,128)S(1)}, s32[4,64]{1,0:T(4,128)}, u32[]{:S(2)}) copy-start(s32[4,64]{1,0:T(4,128)} %mask_hbm.1) | copy-start | bytes 3076
  0.0 0.7 %copy-start = (s32[4,64]{1,0:T(4,128)S(1)}, s32[4,64]{1,0:T(4,128)}, u32[]{:S(2)}) copy-start(s32[4,64]{1,0:T(4,128)} %list_hbm.1) | copy-start | bytes 3076

commit v5 on v4

--- a/solution.py
+++ b/solution.py
@@ -187,32 +187,35 @@
     l_ref[...] = jnp.sum(wt, axis=0, keepdims=True)
     acc[...] = weigh(fb[1], wt)
 
-    @pl.loop(0, 4)
+    @pl.loop(0, 8)
     def _(n):
-        @pl.when(n % 2 == 0)
+        phase, pair = n // 2, n % 2
+
+        @pl.when(phase % 2 == 0)
         def _():
-            for j in range(4):
-                @pl.when(n + j > 0)
+            for j in range(2):
+                slot = 2 * phase + 2 * pair + j
+
+                @pl.when(slot > 0)
                 def _():
-                    pages_in(2 * n + j).wait_recv()
-                    forward(2 * n + j).start()
-
-        @pl.when(n % 2 == 1)
+                    pages_in(slot).wait_recv()
+                    forward(slot).start()
+
+        @pl.when(phase % 2 == 1)
         def _():
-            for j in range(4):
-                forward(2 * (n - 1) + j).wait_recv()
-
-        first = (n % 2) * 8 + (n // 2) * 4
-        slots = pl.ds(first, 4)
-        sc = scores(kvb[0, slots].reshape(512, 128))
-        sc = (sc.reshape(4, 128, 640) + bias[slots]).reshape(512, 640)
+            for j in range(2):
+                forward(2 * (phase - 1) + 2 * pair + j).wait_recv()
+
+        slots = pl.ds((phase % 2) * 8 + (phase // 2) * 4 + 2 * pair, 2)
+        sc = scores(kvb[0, slots].reshape(256, 128))
+        sc = (sc.reshape(2, 128, 640) + bias[slots]).reshape(256, 640)
         old = m_ref[...]
         top = jnp.maximum(old, jnp.max(sc, axis=0, keepdims=True))
         keep = jnp.exp2(old - top)
         wt = jnp.exp2(sc - top)
         m_ref[...] = top
         l_ref[...] = l_ref[...] * keep + jnp.sum(wt, axis=0, keepdims=True)
-        acc[...] = acc[...] * keep + weigh(kvb[1, slots].reshape(512, 128), wt)
+        acc[...] = acc[...] * keep + weigh(kvb[1, slots].reshape(256, 128), wt)
 
     def pieces(x, n):
         out = []
@@ -282,7 +285,7 @@
         for i in range(2):
             total = jnp.zeros((40, 128), F32)
             for k in range(16 * i, 16 * i + 16):
-                total = total + accr[k, 0:40].astype(F32) * factor[0:40, k : k + 1]
+                total = total + accr[k].astype(F32)[0:40] * factor[0:40, k : k + 1]
             attp[i] = jnp.concatenate([total, jnp.zeros((8, 128), F32)], axis=0).astype(BF)
         for dz in (4, 3, 5, 2, 6, 1, 7):
             piece_to(dz).start()

time: 40.3 us -> 40.4 us (level)
  no operation moved by 1% of the time
where the time goes in v5:
time: 40.4 us; the launch traced here: 39.8 us
  Pallas kernels  38.5 us (95%)
  local copies, waits for them, and re-layouts  1.3 us (3%)
    pallas_call x1, Pallas kernels, on_device(): pl.pallas_call(kernel, out_shape=jax.ShapeDtypeStruct((64, 80), BF), in_s...  38.5 us
    unnamed x5, local copies, waits for them, and re-layouts  1.3 us

profile of v5, /device:TPU:4, one launch (start us, length us, event | category | flops | bytes accessed | tf_op | source)
XLA Modules:
  0.0 39.8 jit_solution(5863995046710904115)
XLA Ops:
  0.0 0.0 copy-start.1
  0.0 0.0 copy-start
  0.0 0.7 %copy-done.1 = s32[4,64]{1,0:T(4,128)S(1)} copy-done((s32[4,64]{1,0:T(4,128)S(1)}, s32[4,64]{1,0:T(4,128)}, u32[]{:S(2)}) %copy-start.1) | copy-done | bytes 1048
  0.7 0.0 copy-done
  0.7 38.5 %attend.1 = bf16[64,80]{1,0:T(8,128)(2,1)S(1)} custom-call(bf16[64,5120]{1,0:T(8,128)(2,1)} %bitcast.5, bf16[2,64,1024]{2,1,0:T(8,128)(2,1)} %bitcast.7, bf16[2,128,1024]{2,1,0:T(8,128)(2,1)} %bitcast.6, s32[4,64]{1,0:T(4,128)S(1)} %copy-done, s32[4,64]{1,0:T(4,128)S(1)} %copy-done.1, bf16[80,5120]{1,0:T(8,128)(2,1)} %w_hbm.1), custom_call_target="tpu_custom_call" | custom-call | tf_op jit(solution)/shard_map/attend/pallas_call | solution.py:354
  39.2 0.6 %copy.8 = bf16[4,16,80]{2,1,0:T(8,128)(2,1)} copy(bf16[4,16,80]{2,1,0:T(8,128)(2,1)S(1)} %bitcast.4) | data formatting | bytes 20480
Async XLA Ops:
  0.0 0.7 %copy-start.1 = (s32[4,64]{1,0:T(4,128)S(1)}, s32[4,64]{1,0:T(4,128)}, u32[]{:S(2)}) copy-start(s32[4,64]{1,0:T(4,128)} %mask_hbm.1) | copy-start | bytes 3076
  0.0 0.7 %copy-start = (s32[4,64]{1,0:T(4,128)S(1)}, s32[4,64]{1,0:T(4,128)}, u32[]{:S(2)}) copy-start(s32[4,64]{1,0:T(4,128)} %list_hbm.1) | copy-start | bytes 3076

commit v6 on v5

--- a/solution.py
+++ b/solution.py
@@ -313,9 +313,9 @@
             for i in range(2):
                 os[k, i, :, 0:80] = proj[64 * i : 64 * i + 64, 80 * k : 80 * k + 80]
         for j in range(7, -1, -1):
-            out_to(j, 0).start()
             if j:
                 out_to(j, 1).start()
+            out_to(j, 0).start()
         orv[0] = os[2 * y + l, 1]
 
     result = jnp.zeros((64, 128), F32)

time: 40.4 us -> 40.1 us (level); the launches traced: 39.8 us -> 40 us
  no operation moved by 1% of the time
where the time goes in v6:
time: 40.1 us; the launch traced here: 40 us
  Pallas kernels  38.7 us (97%)
  local copies, waits for them, and re-layouts  1.3 us (3%)
    pallas_call x1, Pallas kernels, on_device(): pl.pallas_call(kernel, out_shape=jax.ShapeDtypeStruct((64, 80), BF), in_s...  38.7 us
    unnamed x5, local copies, waits for them, and re-layouts  1.3 us

profile of v6, /device:TPU:4, one launch (start us, length us, event | category | flops | bytes accessed | tf_op | source)
XLA Modules:
  0.0 40.0 jit_solution(13060507074033597242)
XLA Ops:
  0.0 0.0 copy-start.1
  0.0 0.0 copy-start
  0.0 0.7 %copy-done.1 = s32[4,64]{1,0:T(4,128)S(1)} copy-done((s32[4,64]{1,0:T(4,128)S(1)}, s32[4,64]{1,0:T(4,128)}, u32[]{:S(2)}) %copy-start.1) | copy-done | bytes 1048
  0.7 0.0 copy-done
  0.7 38.7 %attend.1 = bf16[64,80]{1,0:T(8,128)(2,1)S(1)} custom-call(bf16[64,5120]{1,0:T(8,128)(2,1)} %bitcast.5, bf16[2,64,1024]{2,1,0:T(8,128)(2,1)} %bitcast.7, bf16[2,128,1024]{2,1,0:T(8,128)(2,1)} %bitcast.6, s32[4,64]{1,0:T(4,128)S(1)} %copy-done, s32[4,64]{1,0:T(4,128)S(1)} %copy-done.1, bf16[80,5120]{1,0:T(8,128)(2,1)} %w_hbm.1), custom_call_target="tpu_custom_call" | custom-call | tf_op jit(solution)/shard_map/attend/pallas_call | solution.py:354
  39.4 0.6 %copy.8 = bf16[4,16,80]{2,1,0:T(8,128)(2,1)} copy(bf16[4,16,80]{2,1,0:T(8,128)(2,1)S(1)} %bitcast.4) | data formatting | bytes 20480
Async XLA Ops:
  0.0 0.7 %copy-start.1 = (s32[4,64]{1,0:T(4,128)S(1)}, s32[4,64]{1,0:T(4,128)}, u32[]{:S(2)}) copy-start(s32[4,64]{1,0:T(4,128)} %mask_hbm.1) | copy-start | bytes 3076
  0.0 0.7 %copy-start = (s32[4,64]{1,0:T(4,128)S(1)}, s32[4,64]{1,0:T(4,128)}, u32[]{:S(2)}) copy-start(s32[4,64]{1,0:T(4,128)} %list_hbm.1) | copy-start | bytes 3076
